TPU v7x, 32 devices: a whole 2x2x4 slice. The times are simulated.
32 devices in a mesh: groups: 2 (over x), dp: 4 (over z), tensor: 4 (over y, core).
Axes of the slice: x: 2, y: 2, z: 4, core: 2. Of those that a mesh axis runs over, the one named last changes fastest.
Arguments:
- hidden_input: bfloat16 [4096, 5120], P(('groups', 'dp', 'tensor')), parts along dimension 0, may hold values from -0.119628906 to 0.119628906
- query_gradient: bfloat16 [4096, 8192], P(('groups', 'dp'), 'tensor'), parts along dimension 0, may hold values from -6 to 6
- weight: bfloat16 [5120, 8192], P(None, 'tensor'), may hold values from -0.078125 to 0.078125
- adapter_down: bfloat16 [8, 5120, 64], P(None, 'tensor'), may hold values from -0.078125 to 0.078125
- adapter_up: bfloat16 [8, 64, 8192], P(None, None, 'tensor'), may hold values from -0.0625 to 0.0625
- live_per_block: int32 [32], P(('groups', 'dp')), parts along dimension 0, may hold values from 1 to 128, 1536 in all
- adapter_per_block: int32 [32, 1], P(('groups', 'dp')), parts along dimension 0, may hold values from 0 to 7
Outputs:
- hidden_gradient: bfloat16 [4096, 5120], P(('groups', 'dp', 'tensor')), parts along dimension 0
- grad_down: float32 [16, 5120, 64], P(('groups', 'dp'), 'tensor'), parts along dimension 0
- grad_up: float32 [16, 64, 8192], P(('groups', 'dp'), None, 'tensor'), parts along dimension 0
There are 2 independent parts, one for each index of `groups`. A program takes and returns all parts, laid end to end along the dimension named above; an argument that names none is the same for every part. Nothing has to cross between parts.
Inputs may be any that keep to these rules, and one draw needn't show every extreme that they name: live_per_block gives how many rows at the head of a block of 128 rows are live; some block is full. `adapter_per_block`: every adapter owns some block.
All inputs are finite; a program needn't handle non-finite values.
Results may differ from a plain program's by a relative error of at most 0.015.
Values may be sent and summed in bfloat16 or wider, within the bound.
A program may use at most 128 MiB of HBM per device.

v0:
```python
import jax
import jax.numpy as jnp
from jax import lax
from jax.sharding import PartitionSpec as P

BLOCK = 128


adapter_scale = 2.0


def on_device(
    hidden_input,
    query_gradient,
    weight,
    adapter_down,
    adapter_up,
    live_per_block,
    adapter_per_block,
):
    token_rows_local = hidden_input.shape[0]
    group = query_gradient.shape[0]
    nblocks = group // BLOCK
    q_local = query_gradient.shape[1]
    local_width = adapter_down.shape[1]
    adapter_list = adapter_down.shape[0]
    positions = jnp.arange(BLOCK, dtype=jnp.int32)
    live = (positions[None, :] < live_per_block[:, None]).astype(jnp.bfloat16)
    masked_rows = query_gradient.reshape(nblocks, BLOCK, q_local) * live[:, :, None]
    adapter_index = adapter_per_block[:, 0]
    columns = lax.all_to_all(hidden_input, "tensor", split_axis=1, concat_axis=0, tiled=True)
    column_blocks = columns.reshape(nblocks, BLOCK, local_width)
    down_block_list = adapter_down[adapter_index]
    up_block_list = adapter_up[adapter_index]
    grad_part = jnp.einsum(
        "bkq,brq->bkr", masked_rows, up_block_list, preferred_element_type=jnp.float32
    )
    act_part = jnp.einsum(
        "shu,sup->shp", column_blocks, down_block_list, preferred_element_type=jnp.float32
    )
    grad_sum, act_sum = (
        lax.psum(grad_part.astype(jnp.bfloat16), "tensor").astype(jnp.float32),
        lax.psum(act_part.astype(jnp.bfloat16), "tensor").astype(jnp.float32),
    )
    rank_gradient = grad_sum.astype(jnp.bfloat16)
    act_low = act_sum.astype(jnp.bfloat16)
    flat = masked_rows.reshape(group, q_local)
    frozen_gradient = lax.psum_scatter(
        lax.dot_general(
            flat, weight, (((1,), (1,)), ((), ())), preferred_element_type=jnp.float32
        ).astype(jnp.bfloat16),
        "tensor",
        scatter_dimension=0,
        tiled=True,
    ).astype(jnp.float32)
    complete_down = lax.all_gather(adapter_down, "tensor", axis=1, tiled=True)
    own_count = token_rows_local // BLOCK
    first = lax.axis_index("tensor") * own_count
    local_gradient = lax.dynamic_slice_in_dim(rank_gradient, first, own_count, 0)
    local_index = lax.dynamic_slice_in_dim(adapter_index, first, own_count, 0)
    local_rows = adapter_scale * jnp.einsum(
        "lqm,lsm->lqs",
        local_gradient,
        complete_down[local_index],
        preferred_element_type=jnp.float32,
    )
    adapter_rows = local_rows.astype(jnp.bfloat16).reshape(token_rows_local, hidden_input.shape[1])
    hidden_gradient = (frozen_gradient + adapter_rows.astype(jnp.float32)).astype(jnp.bfloat16)
    down_terms = jnp.einsum(
        "mfq,mfc->mqc", column_blocks, rank_gradient, preferred_element_type=jnp.float32
    )
    up_terms = jnp.einsum("bkr,bkq->brq", act_low, masked_rows, preferred_element_type=jnp.float32)
    selector = (
        adapter_index[None, :] == jnp.arange(adapter_list, dtype=jnp.int32)[:, None]
    ).astype(jnp.float32)
    down_total = adapter_scale * jnp.einsum(
        "ab,bdr->adr", selector, down_terms, precision=lax.Precision.HIGHEST
    )
    up_total = adapter_scale * jnp.einsum(
        "ab,brq->arq", selector, up_terms, precision=lax.Precision.HIGHEST
    )
    grad_down, grad_up = (
        lax.psum_scatter(
            down_total.astype(jnp.bfloat16), "dp", scatter_dimension=0, tiled=True
        ).astype(jnp.float32),
        lax.psum_scatter(
            up_total.astype(jnp.bfloat16), "dp", scatter_dimension=0, tiled=True
        ).astype(jnp.float32),
    )
    return (hidden_gradient, grad_down, grad_up)


def solution(mesh):
    return jax.shard_map(
        on_device,
        mesh=mesh,
        in_specs=(
            P(("groups", "dp", "tensor"), None),
            P(("groups", "dp"), "tensor"),
            P(None, "tensor"),
            P(None, "tensor", None),
            P(None, None, "tensor"),
            P(("groups", "dp")),
            P(("groups", "dp"), None),
        ),
        out_specs=(
            P(("groups", "dp", "tensor"), None),
            P(("groups", "dp"), "tensor", None),
            P(("groups", "dp"), None, "tensor"),
        ),
        check_vma=False,
    )
```

profile of v0, /device:TPU:0, one launch (start us, length us, event | category | flops | bytes accessed | tf_op | source)
XLA Modules:
  0.0 253.2 jit_solution(3850341454648822367)
XLA Ops:
  7.2 0.0 copy-start
  7.2 1.9 copy.14
  9.1 0.0 copy-start.2
  9.1 1.4 copy.15
  10.6 4.2 %all-to-all-start = ((bf16[128,4,1280]{2,0,1:T(8,128)(2,1)}), bf16[128,4,1280]{2,0,1:T(8,128)(2,1)S(1)}, u32[]{:S(2)}, u32[]{:S(2)}) async-start(bf16[128,4,1280]{2,0,1:T(8,128)(2,1)} %copy.15), calls=%async_computation.1 | async-start | bytes 2621440 | tf_op jit(solution)/shard_map/all_to_all | solution.py:31
  14.8 0.0 all-reduce.3.cloned.1.call-start
  14.8 0.0 copy-done.2
  14.8 0.0 copy-done
  14.8 0.0 copy-start.3
  14.8 1.6 gather_fusion
  16.4 2.7 %gather_fusion.1 = bf16[4,1280,64]{1,2,0:T(8,128)(2,1)} fusion(bf16[8,1280,64]{1,2,0:T(8,128)(2,1)} %param.10, s32[1024]{0:T(1024)S(1)} %pad_clamp_fusion), kind=kCustom, calls=%fused_computation.1 | custom fusion | bytes 1310736 | tf_op jit(solution)/shard_map/gather | solution.py:33
  19.2 0.0 copy-done.3
  19.2 0.1 fusion.31
  19.2 3.4 %fusion.18 = bf16[4,128,64]{1,2,0:T(8,128)(2,1)} fusion(bf16[4,64,2048]{2,1,0:T(8,128)(2,1)} %gather_fusion, bf16[4,128,2048]{2,1,0:T(8,128)(2,1)} %bitcast.38, bf16[4,128]{1,0:T(4,128)(2,1)S(1)} %get-tuple-element.19), kind=kOutput, calls=%fused_computation.23 | convolution fusion | flops 135299072 | bytes 3212288 | tf_op jit(solution)/shard_map/bkq,brq->bkr/dot_general | solution.py:35
  22.6 9.4 %all-to-all-done = bf16[128,4,1280]{2,0,1:T(8,128)(2,1)S(1)} async-done(((bf16[128,4,1280]{2,0,1:T(8,128)(2,1)}), bf16[128,4,1280]{2,0,1:T(8,128)(2,1)S(1)}, u32[]{:S(2)}, u32[]{:S(2)}) %all-to-all-start) | async-done | bytes 1310752 | tf_op jit(solution)/shard_map/all_to_all | solution.py:31
  32.1 2.3 fusion.21
  34.3 0.0 all-reduce.3.cloned.1.call-update
  34.4 0.0 reduce-scatter.6.cloned.1.call-start
  34.4 32.7 %all-reduce.3.cloned.1.call-done = (bf16[4,128,64]{1,2,0:T(8,128)(2,1)}, bf16[4,128,64]{1,2,0:T(8,128)(2,1)}) async-done(((bf16[4,128,64]{1,2,0:T(8,128)(2,1)}, bf16[4,128,64]{1,2,0:T(8,128)(2,1)}), (bf16[4,128,64]{1,2,0:T(8,128)(2,1)}, bf16[4,128,64]{1,2,0:T(8,128)(2,1)})) %all-reduce.3.cloned.1.call-update) | async-done | bytes 131088 | tf_op jit(solution)/shard_map/psum | solution.py:42
  67.1 1.2 convolution_bitcast_fusion
  68.2 2.4 fusion.4
  70.7 0.0 copy-start.1
  70.7 1.3 copy.17
  72.0 0.0 reduce-scatter.6.cloned.1.call-update
  72.0 0.0 reduce-scatter.8.cloned.1.call-start
  72.0 0.0 copy-done.1
  72.1 2.1 fusion.7
  74.2 3.5 %multiply_convert_fusion = bf16[8,64,2048]{2,0,1:T(8,128)(2,1)S(1)} fusion(f32[4,64,2048]{2,1,0:T(8,128)S(1)} %fusion.7, s32[4]{0:T(128)S(1)} %bitcast.41), kind=kOutput, calls=%fused_computation.8 | convolution fusion | flops 52428832 | bytes 4194320 | tf_op jit(solution)/shard_map/ab,brq->arq/dot_general | solution.py:79
  77.6 2.5 copy.19
  80.1 0.0 reduce-scatter.8.cloned.1.call-update
  80.1 0.0 all-gather.2.cloned.1.call-start
  80.2 0.5 all-gather.2.cloned.1.call-update
  80.7 0.2 reduce-scatter.4.cloned.1.call-start
  80.9 17.5 %convolution_convert_fusion = bf16[512,5120]{1,0:T(8,128)(2,1)} fusion(bf16[5120,2048]{1,0:T(8,128)(2,1)} %param.9, bf16[512,2048]{1,0:T(8,128)(2,1)} %param.8, bf16[512]{0:T(512)(128)(2,1)S(1)} %get-tuple-element.20), kind=kOutput, calls=%fused_computation.2 | convolution fusion | flops 10741088256 | bytes 28312576 | tf_op jit(solution)/shard_map/dot_general | solution.py:49
  98.4 0.0 reduce-scatter.4.cloned.1.call-update
  98.4 0.6 constant_dynamic-slice_fusion
  101.0 2.4 reduce-scatter.6.cloned.1.call-done
  103.4 1.9 convert_element_type.65
  105.2 43.3 %reduce-scatter.8.cloned.1.call-done = bf16[2,64,2048]{2,1,0:T(8,128)(2,1)} async-done(((bf16[8,64,2048]{2,1,0:T(8,128)(2,1)}), bf16[2,64,2048]{2,1,0:T(8,128)(2,1)}) %reduce-scatter.8.cloned.1.call-update) | async-done | bytes 524304 | tf_op jit(solution)/shard_map/reduce_scatter | solution.py:86
  148.5 2.1 convert_element_type.69
  150.6 39.1 %all-gather.2.cloned.1.call-done = bf16[8,5120,64]{1,2,0:T(8,128)(2,1)} async-done(((bf16[8,1280,64]{1,2,0:T(8,128)(2,1)}), bf16[8,5120,64]{1,2,0:T(8,128)(2,1)}) %all-gather.2.cloned.1.call-update) | async-done | bytes 5242896 | tf_op jit(solution)/shard_map/all_gather | solution.py:56
  189.7 53.8 %reduce-scatter.4.cloned.1.call-done = bf16[128,5120]{1,0:T(8,128)(2,1)} async-done(((bf16[512,5120]{1,0:T(8,128)(2,1)}), bf16[128,5120]{1,0:T(8,128)(2,1)}) %reduce-scatter.4.cloned.1.call-update) | async-done | bytes 1310736 | tf_op jit(solution)/shard_map/reduce_scatter | solution.py:48
  243.5 3.1 %fusion.3 = bf16[128,5120]{1,0:T(8,128)(2,1)} fusion(bf16[128,5120]{1,0:T(8,128)(2,1)} %reduce-scatter.4.cloned.1.call-done, bf16[8,5120,64]{1,2,0:T(8,128)(2,1)} %all-gather.2.cloned.1.call-done, s32[]{:T(128)} %bitcast.5, bf16[4,128,64]{1,2,0:T(8,128)(2,1)} %get-tuple-element.17, s32[]{:T(128)S(6)} %select_n.13), kind=kOutput, calls=%fused_computation.7 | convolution fusion | flops 87818240 | bytes 3293700 | tf_op jit(solution)/shard_map/lqm,lsm->lqs/dot_general | solution.py:61
  (2 shorter events, 0.0 us)
Async XLA Ops:
  7.2 7.7 %copy-start = (bf16[8,64,2048]{2,1,0:T(8,128)(2,1)S(1)}, bf16[8,64,2048]{2,1,0:T(8,128)(2,1)}, u32[]{:S(2)}) copy-start(bf16[8,64,2048]{2,1,0:T(8,128)(2,1)} %param.11) | copy-start | bytes 6291460
  9.1 5.7 %copy-start.2 = (s32[4,1]{0,1:T(1,128)S(1)}, s32[4,1]{0,1:T(1,128)}, u32[]{:S(2)}) copy-start(s32[4,1]{0,1:T(1,128)} %param.13) | copy-start | bytes 52
  10.6 21.5 %all-to-all-start = ((bf16[128,4,1280]{2,0,1:T(8,128)(2,1)}), bf16[128,4,1280]{2,0,1:T(8,128)(2,1)S(1)}, u32[]{:S(2)}, u32[]{:S(2)}) async-start(bf16[128,4,1280]{2,0,1:T(8,128)(2,1)} %copy.15), calls=%async_computation.1 | async-start | bytes 2621440 | tf_op jit(solution)/shard_map/all_to_all | solution.py:31
  14.8 52.3 %all-reduce.3.cloned.1.call-start = ((), (), s32[]{:S(2)}) async-start(), calls=%async_computation.8 | async-start | bytes 262144 | tf_op jit(solution)/shard_map/psum | solution.py:42
  14.8 4.3 %copy-start.3 = (s32[4]{0:T(128)S(1)}, s32[4]{0:T(128)}, u32[]{:S(2)}) copy-start(s32[4]{0:T(128)} %param.12) | copy-start | bytes 52
  34.4 69.0 %reduce-scatter.6.cloned.1.call-start = ((), (), s32[]{:S(2)}) async-start(), calls=%async_computation.6 | async-start | bytes 1638400 | tf_op jit(solution)/shard_map/reduce_scatter | solution.py:83
  70.7 1.4 copy-start.1
  72.0 76.5 %reduce-scatter.8.cloned.1.call-start = ((), (), s32[]{:S(2)}) async-start(), calls=%async_computation.7 | async-start | bytes 2621440 | tf_op jit(solution)/shard_map/reduce_scatter | solution.py:86
  80.1 109.6 %all-gather.2.cloned.1.call-start = ((), (), s32[]{:S(2)}) async-start(), calls=%async_computation.5 | async-start | bytes 6553600 | tf_op jit(solution)/shard_map/all_gather | solution.py:56
  80.7 162.8 %reduce-scatter.4.cloned.1.call-start = ((), (), s32[]{:S(2)}) async-start(), calls=%async_computation.4 | async-start | bytes 6553600 | tf_op jit(solution)/shard_map/reduce_scatter | solution.py:48
Sparse Core Ops, SparseCore 0:
  34.5 32.5 all-reduce.2
  72.1 31.1 reduce-scatter.5
  105.8 42.6 reduce-scatter.7
  149.9 39.7 all-gather.1
  192.1 51.3 reduce-scatter.3
where the time goes:
time: 254 us; the launch traced here: 253 us
  waiting for transfers between devices  181 us (71%)
  matrix products  35.4 us (14%)
  between operations  15.8 us (6%)
  local copies, waits for them, and re-layouts  12 us (5%)
  starting transfers between devices  4.58 us (2%)
  other arithmetic  4.05 us (2%)
    reduce_scatter x1, waiting for transfers between devices, on_device(): lax.psum_scatter(lax.dot_general(flat, weight, (((1,), (1,)), ((), ())),...  53.8 us
    reduce_scatter x1, waiting for transfers between devices, on_device(): lax.psum_scatter(up_total.astype(jnp.bfloat16), 'dp', scatter_dimension=0...  43.3 us
    all_gather x1, waiting for transfers between devices, on_device(): complete_down = lax.all_gather(adapter_down, 'tensor', axis=1, tiled=True)  39.1 us
    psum x1, waiting for transfers between devices, on_device(): lax.psum(grad_part.astype(jnp.bfloat16), 'tensor').astype(jnp.float32)  32.7 us
    dot_general x1, matrix products, on_device(): lax.dot_general(flat, weight, (((1,), (1,)), ((), ())), preferred_element...  17.5 us
    all_to_all x1, waiting for transfers between devices, on_device(): lax.all_to_all(hidden_input, 'tensor', split_axis=1, concat_axis=0, tiled...  9.44 us
  transfers between devices with their start and end apart: 6, of which 6 were waited for; matrix products, arithmetic and copies ran while one was open for 15% of the time, Pallas kernels for 0%

commit v1 on v0

--- a/solution.py
+++ b/solution.py
@@ -1,12 +1,410 @@
 import jax
 import jax.numpy as jnp
 from jax import lax
+from jax.experimental import pallas as pl
+from jax.experimental.pallas import tpu as pltpu
 from jax.sharding import PartitionSpec as P
 
 BLOCK = 128
+MESH = pl.DeviceIdType.MESH
+F32, BF16 = jnp.float32, jnp.bfloat16
 
 
 adapter_scale = 2.0
+UP_CHUNKS, DOWN_CHUNKS, STEP, WBUFS = 4, 2, 256, 3
+
+
+def dot_nt(a, b):
+    return lax.dot_general(a, b, (((1,), (1,)), ((), ())), preferred_element_type=F32)
+
+
+def dot_nn(a, b):
+    return lax.dot_general(a, b, (((1,), (0,)), ((), ())), preferred_element_type=F32)
+
+
+def dot_tn(a, b):
+    return lax.dot_general(a, b, (((0,), (0,)), ((), ())), preferred_element_type=F32)
+
+
+def kernel(
+    live_ref, idx_ref, hid_ref, g_ref, w_ref, down_ref, up_ref,
+    hg_ref, gd_ref, gu_ref,
+    m_g, w_buf, up_v, down_v, cols, pf, acc, core_s, core_r, y_s, y_r, lora,
+    lg_s, lg_r, la_s, la_r, low_g, low_a, lhs, slots_d, slots_u,
+    s1d, s1u, td, tu, xd, xu, s2d, s2u, fd, fu, ids_s, ids_r, sel,
+    loc_sem, w_sem, hs_sem, hr_sem, lgs_sem, lgr_sem, las_sem, lar_sem,
+    cs_sem, cr_sem, ys_sem, yr_sem,
+    s1_sem, t_sem, x_sem, s2_sem, f_sem, id_sem,
+):
+    d = lax.axis_index("dp")
+    t = lax.axis_index("tensor")
+    y, c = t // 2, t % 2
+    core_peer = y * 2 + (1 - c)
+    y_peer = (1 - y) * 2 + c
+    is_mid = jnp.logical_or(d == 1, d == 2)
+    is_end = jnp.logical_not(is_mid)
+    low_side = d < 2
+    outer = jnp.where(low_side, 0, 3)
+    inner = jnp.where(low_side, 1, 2)
+    cross = jnp.where(low_side, 2, 1)
+    far = 3 - outer
+    nb = 4
+    own, rank = gd_ref.shape[0] // 64, 64
+    width = down_v.shape[2]
+    q = m_g.shape[1]
+    uw, dw = q // UP_CHUNKS, width // DOWN_CHUNKS
+
+    loads = [
+        pltpu.make_async_copy(g_ref, m_g, loc_sem.at[0]),
+        pltpu.make_async_copy(up_ref, up_v, loc_sem.at[1]),
+        pltpu.make_async_copy(hid_ref.at[:, pl.ds(pl.multiple_of(t * width, 128), width)],
+                              cols.at[pl.ds(pl.multiple_of(t * BLOCK, BLOCK), BLOCK), :], loc_sem.at[2]),
+        pltpu.make_async_copy(down_ref, down_v, loc_sem.at[3]),
+    ]
+    for x in loads[:2]:
+        x.start()
+
+    def w_load(j):
+        return pltpu.make_async_copy(
+            w_ref.at[pl.ds(j * width, width), :], w_buf.at[j % WBUFS], w_sem.at[j]
+        )
+
+    w_load(0).start()
+    loads[2].start()
+    loads[3].start()
+    for j in range(1, WBUFS):
+        w_load(j).start()
+
+    barrier = pltpu.get_barrier_semaphore()
+    for r in range(1, 4):
+        pl.semaphore_signal(barrier, inc=1, device_id={"tensor": lax.rem(t + r, 4)}, device_id_type=MESH)
+
+    @pl.when(is_mid)
+    def _():
+        pl.semaphore_signal(barrier, inc=1, device_id={"dp": outer}, device_id_type=MESH)
+        pl.semaphore_signal(barrier, inc=1, device_id={"dp": cross}, device_id_type=MESH)
+        pl.semaphore_wait(barrier, 5)
+
+    @pl.when(is_end)
+    def _():
+        pl.semaphore_signal(barrier, inc=1, device_id={"dp": inner}, device_id_type=MESH)
+        pl.semaphore_wait(barrier, 4)
+
+    def remote(src, dst, ssem, rsem, dev):
+        return pltpu.make_async_remote_copy(
+            src_ref=src, dst_ref=dst, send_sem=ssem, recv_sem=rsem, device_id=dev, device_id_type=MESH
+        )
+
+    def rows_of(b):
+        return pl.ds(pl.multiple_of(b * BLOCK, BLOCK), BLOCK)
+
+    def hid_copy(r, sender):
+        p = lax.rem(t + r, 4)
+        return remote(
+            hid_ref.at[:, pl.ds(pl.multiple_of(p * width, 128), width)],
+            cols.at[rows_of(sender), :], hs_sem.at[r], hr_sem.at[r], {"tensor": p},
+        )
+
+    for r in range(1, 4):
+        hid_copy(r, t).start()
+
+    lane = lax.broadcasted_iota(jnp.int32, ids_s.shape, 1) // rank
+    ids = jnp.zeros(ids_s.shape, F32)
+    for b in range(nb):
+        ids = ids + jnp.where(lane == b, 1.0, 0.0) * idx_ref[b].astype(F32)
+    ids_s[...] = ids
+
+    @pl.when(is_end)
+    def _():
+        remote(ids_s, ids_r, id_sem.at[0], id_sem.at[1], {"dp": inner}).start()
+
+    loads[0].wait()
+    loads[1].wait()
+    for b in range(nb):
+        keep = (lax.broadcasted_iota(jnp.int32, (BLOCK, 1), 0) < live_ref[b]).astype(F32)
+        rows = (m_g[pl.ds(b * BLOCK, BLOCK), :].astype(F32) * keep).astype(BF16)
+        m_g[pl.ds(b * BLOCK, BLOCK), :] = rows
+        lg_s[:, pl.ds(b * BLOCK, BLOCK)] = dot_nt(up_v[idx_ref[b]], rows).astype(BF16)
+
+    def low_copy(buf_s, buf_r, ssem, rsem, r):
+        return remote(buf_s, buf_r.at[r - 1], ssem.at[r], rsem.at[r], {"tensor": lax.rem(t + r, 4)})
+
+    for r in range(1, 4):
+        low_copy(lg_s, lg_r, lgs_sem, lgr_sem, r).start()
+
+    def partial(j):
+        w_load(j).wait()
+
+        def body(n, carry):
+            at = pl.ds(pl.multiple_of(n * STEP, STEP), STEP)
+            pf[j % 2, :, at] = dot_nt(m_g[...], w_buf[j % WBUFS, at, :])
+            return carry
+
+        lax.fori_loop(0, width // STEP, body, 0)
+        if j + WBUFS < 4:
+            w_load(j + WBUFS).start()
+
+    def core_copy(j):
+        return remote(core_s.at[j], core_r.at[j], cs_sem.at[j], cr_sem.at[j], {"tensor": core_peer})
+
+    def y_copy(j):
+        return remote(y_s.at[j], y_r.at[j], ys_sem.at[j], yr_sem.at[j], {"tensor": y_peer})
+
+    def send_core(j):
+        @pl.when(t == j)
+        def _():
+            for b in range(nb):
+                at = pl.ds(b * BLOCK, BLOCK)
+                pf[j % 2, at, :] = pf[j % 2, at, :] + lora[at, :].astype(F32)
+
+        for k in range(2):
+            core_s[j, k] = pf[j % 2, rows_of(2 * k + 1 - c), :].astype(BF16)
+        core_copy(j).start()
+
+    def combine(j):
+        core_copy(j).wait_recv()
+        y_s[j] = (pf[j % 2, rows_of((1 - y) * 2 + c), :] + core_r[j, 1 - y].astype(F32)).astype(BF16)
+        y_copy(j).start()
+        acc[:, pl.ds(j * width, width)] = pf[j % 2, rows_of(y * 2 + c), :] + core_r[j, y].astype(F32)
+
+    partial(0)
+    partial(1)
+
+    for r in range(1, 4):
+        low_copy(lg_s, lg_r, lgs_sem, lgr_sem, r).wait_recv()
+    low_g[...] = (
+        lg_s[...].astype(F32) + lg_r[0].astype(F32) + lg_r[1].astype(F32) + lg_r[2].astype(F32)
+    ).astype(BF16)
+    loads[3].wait()
+    for b in range(nb):
+        at = pl.ds(b * BLOCK, BLOCK)
+        lora[at, :] = (adapter_scale * dot_tn(low_g[:, at], down_v[idx_ref[b]])).astype(BF16)
+    send_core(0)
+    send_core(1)
+
+    loads[2].wait()
+    for r in range(1, 4):
+        hid_copy(r, lax.rem(t + 4 - r, 4)).wait_recv()
+    for b in range(nb):
+        at = pl.ds(b * BLOCK, BLOCK)
+        la_s[:, at] = dot_nt(down_v[idx_ref[b]], cols[at, :]).astype(BF16)
+    for r in range(1, 4):
+        low_copy(la_s, la_r, las_sem, lar_sem, r).start()
+
+    end_f = is_end.astype(F32)
+
+    def adapter_of(s):
+        if s < own:
+            return cross * own + s
+        if s < 2 * own:
+            return far * own + (s - own)
+        if s < 3 * own:
+            return d * own + (s - 2 * own)
+        return outer * own + (s - 3 * own)
+
+    def fill(low):
+        for s in range(4 * own):
+            for b in range(nb):
+                same = (idx_ref[b] == adapter_of(s)).astype(F32)
+                if s < 2 * own:
+                    same = end_f * (1.0 if s == b else 0.0) + (1.0 - end_f) * same
+                at = pl.ds(b * BLOCK, BLOCK)
+                lhs[pl.ds(s * rank, rank), at] = (low[:, at].astype(F32) * (adapter_scale * same)).astype(BF16)
+
+    NC = DOWN_CHUNKS + UP_CHUNKS
+
+    def pick(k, down, up):
+        return down.at[k] if k < DOWN_CHUNKS else up.at[k - DOWN_CHUNKS]
+
+    def slot_at(k):
+        if k < DOWN_CHUNKS:
+            return slots_d, pl.ds(k * dw, dw)
+        return slots_u, pl.ds((k - DOWN_CHUNKS) * uw, uw)
+
+    def end_copy(k):
+        return remote(pick(k, s1d, s1u), pick(k, td, tu), s1_sem.at[k], t_sem.at[k], {"dp": inner})
+
+    def cross_copy(k):
+        return remote(pick(k, s1d, s1u), pick(k, xd, xu), s1_sem.at[k], x_sem.at[k], {"dp": cross})
+
+    def outer_copy(k):
+        return remote(pick(k, s2d, s2u), pick(k, fd, fu), s2_sem.at[k], f_sem.at[k], {"dp": outer})
+
+    half, own_rows, out_rows = 2 * own * rank, own * rank, 3 * own * rank
+
+    def local_terms(k):
+        slots, at = slot_at(k)
+        right = cols if k < DOWN_CHUNKS else m_g
+        slots[:, at] = dot_nn(lhs[...], right[:, at])
+
+        @pl.when(is_end)
+        def _():
+            pick(k, s1d, s1u)[...] = slots[0:half, at].astype(BF16)
+            end_copy(k).start()
+
+    def middle_sums(k):
+        slots, at = slot_at(k)
+
+        @pl.when(is_mid)
+        def _():
+            end_copy(k).wait_recv()
+            more = dot_nn(sel[...], pick(k, td, tu)[...])
+            pick(k, s1d, s1u)[...] = (slots[0:half, at] + more[0:half]).astype(BF16)
+            cross_copy(k).start()
+            slots[half:out_rows, at] = slots[half:out_rows, at] + more[half:]
+
+    def middle_out(k):
+        slots, at = slot_at(k)
+        out = gd_ref if k < DOWN_CHUNKS else gu_ref
+
+        @pl.when(is_mid)
+        def _():
+            cross_copy(k).wait_recv()
+            got = pick(k, xd, xu)
+            pick(k, s2d, s2u)[...] = (slots[out_rows:, at] + got[own_rows:, :].astype(F32)).astype(BF16)
+            outer_copy(k).start()
+            out[:, at] = slots[half:out_rows, at] + got[0:own_rows, :].astype(F32)
+
+    def end_out(k):
+        slots, at = slot_at(k)
+        out = gd_ref if k < DOWN_CHUNKS else gu_ref
+
+        @pl.when(is_end)
+        def _():
+            outer_copy(k).wait_recv()
+            out[:, at] = slots[half:out_rows, at] + pick(k, fd, fu)[...].astype(F32)
+
+    fill(low_g)
+    for k in range(DOWN_CHUNKS):
+        local_terms(k)
+    combine(0)
+    combine(1)
+    partial(2)
+    send_core(2)
+
+    for r in range(1, 4):
+        low_copy(la_s, la_r, las_sem, lar_sem, r).wait_recv()
+    low_a[...] = (
+        la_s[...].astype(F32) + la_r[0].astype(F32) + la_r[1].astype(F32) + la_r[2].astype(F32)
+    ).astype(BF16)
+    fill(low_a)
+    for k in range(DOWN_CHUNKS, NC):
+        local_terms(k)
+
+    @pl.when(is_mid)
+    def _():
+        remote(ids_s, ids_r, id_sem.at[0], id_sem.at[1], {"dp": cross}).wait_recv()
+        eye = lax.broadcasted_iota(jnp.int32, (rank, nb * rank), 0) == (
+            lax.broadcasted_iota(jnp.int32, (rank, nb * rank), 1) % rank
+        )
+        eye = eye.astype(F32)
+        for s in range(3 * own):
+            same = (ids_r[0:1, :] == adapter_of(s).astype(F32)).astype(F32)
+            sel[pl.ds(s * rank, rank), :] = (eye * same).astype(BF16)
+
+    for k in range(DOWN_CHUNKS):
+        middle_sums(k)
+    combine(2)
+    partial(3)
+    send_core(3)
+    middle_sums(DOWN_CHUNKS)
+    combine(3)
+    for k in range(DOWN_CHUNKS):
+        middle_out(k)
+    for k in range(DOWN_CHUNKS + 1, NC):
+        middle_sums(k)
+        middle_out(k - 1)
+    middle_out(NC - 1)
+    for j in range(4):
+        at = pl.ds(j * width, width)
+        y_copy(j).wait_recv()
+        hg_ref[:, at] = (acc[:, at] + y_r[j].astype(F32)).astype(BF16)
+    for k in range(NC):
+        end_out(k)
+
+    for r in range(1, 4):
+        hid_copy(r, t).wait_send()
+        low_copy(lg_s, lg_r, lgs_sem, lgr_sem, r).wait_send()
+        low_copy(la_s, la_r, las_sem, lar_sem, r).wait_send()
+    for j in range(4):
+        core_copy(j).wait_send()
+        y_copy(j).wait_send()
+    for k in range(NC):
+        end_copy(k).wait_send()
+
+    @pl.when(is_mid)
+    def _():
+        for k in range(NC):
+            outer_copy(k).wait_send()
+
+    @pl.when(is_end)
+    def _():
+        remote(ids_s, ids_r, id_sem.at[0], id_sem.at[1], {"dp": inner}).wait_send()
+
+
+def fused(hidden_input, query_gradient, weight, adapter_down, adapter_up, live_per_block, adapter_per_block):
+    down_t = adapter_down.transpose(0, 2, 1)
+    na, rank, width = down_t.shape
+    group, q = query_gradient.shape
+    rows, model = hidden_input.shape
+    own = na // 4
+    nt = 4
+    uw, dw = q // UP_CHUNKS, width // DOWN_CHUNKS
+    half, mine = 2 * own * rank, own * rank
+    V, S = pltpu.VMEM, pltpu.SemaphoreType.DMA
+    nc = UP_CHUNKS + DOWN_CHUNKS
+
+    def pair(height):
+        return [V((DOWN_CHUNKS, height, dw), BF16), V((UP_CHUNKS, height, uw), BF16)]
+
+    any_spec = pl.BlockSpec(memory_space=pl.ANY)
+    smem = pl.BlockSpec(memory_space=pltpu.SMEM)
+    vmem = pl.BlockSpec(memory_space=pltpu.VMEM)
+    hg, gd, gu = pl.pallas_call(
+        kernel,
+        out_shape=(
+            jax.ShapeDtypeStruct((rows, model), BF16),
+            jax.ShapeDtypeStruct((mine, width), F32),
+            jax.ShapeDtypeStruct((mine, q), F32),
+        ),
+        in_specs=[smem, smem] + [any_spec] * 5,
+        out_specs=(vmem,) * 3,
+        scratch_shapes=[
+            V((group, q), BF16),
+            V((WBUFS, width, q), BF16),
+            V((na, rank, q), BF16),
+            V((na, rank, width), BF16),
+            V((group, width), BF16),
+            V((2, group, width), F32),
+            V((rows, model), F32),
+            V((nt, 2, rows, width), BF16),
+            V((nt, 2, rows, width), BF16),
+            V((nt, rows, width), BF16),
+            V((nt, rows, width), BF16),
+            V((group, width), BF16),
+            V((rank, group), BF16),
+            V((3, rank, group), BF16),
+            V((rank, group), BF16),
+            V((3, rank, group), BF16),
+            V((rank, group), BF16),
+            V((rank, group), BF16),
+            V((na * rank, group), BF16),
+            V((na * rank, width), F32),
+            V((na * rank, q), F32),
+        ]
+        + pair(half) + pair(half) + pair(half) + pair(mine) + pair(mine)
+        + [V((8, nt * rank), F32), V((8, nt * rank), F32), V((3 * mine, nt * rank), BF16)]
+        + [S((n,)) for n in (4, 4, 4, 4, 4, 4, 4, 4, 4, 4, 4, 4, nc, nc, nc, nc, nc, 2)],
+        compiler_params=pltpu.CompilerParams(
+            collective_id=0, has_side_effects=True, vmem_limit_bytes=62 * 1024 * 1024
+        ),
+        cost_estimate=pl.CostEstimate(
+            flops=2 * group * q * model, bytes_accessed=2 * model * q, transcendentals=0
+        ),
+    )(
+        live_per_block, adapter_per_block[:, 0], hidden_input, query_gradient, weight, down_t, adapter_up,
+    )
+    return hg, gd.reshape(own, rank, width).transpose(0, 2, 1), gu.reshape(own, rank, q)
 
 
 def on_device(
@@ -91,8 +489,9 @@
 
 
 def solution(mesh):
+    sizes = (mesh.shape["dp"], mesh.shape["tensor"])
     return jax.shard_map(
-        on_device,
+        fused if sizes == (4, 4) else on_device,
         mesh=mesh,
         in_specs=(
             P(("groups", "dp", "tensor"), None),

time: 254 us -> 86.4 us (0.34)
  waiting for transfers between devices: 181 us -> 0 us
  Pallas kernels: 0 us -> 80.5 us
  matrix products: 35.4 us -> 0 us
  between operations: 15.8 us -> 0.65 us
  local copies, waits for them, and re-layouts: 12 us -> 4.96 us
  starting transfers between devices: 4.58 us -> 0 us
  other arithmetic: 4.05 us -> 0 us
    reduce_scatter x3 -> x0, waiting for transfers between devices: 99.5 us -> none  [the longest x1 53.8 us: on_device(): lax.psum_scatter(lax.dot_general(flat, weight, (((1,), (1,)), ((), ())),...]
    pallas_call x0 -> x1, Pallas kernels: none -> 80.5 us  [fused(): pl.pallas_call(kernel, out_shape=(jax.ShapeDtypeStruct((rows, model), BF1...]
    all_gather x1 -> x0, waiting for transfers between devices: 39.1 us -> none  [on_device(): complete_down = lax.all_gather(adapter_down, 'tensor', axis=1, tiled=True)]
    dot_general x8 -> x0, matrix products: 35.4 us -> none  [the longest x1 17.5 us: on_device(): lax.dot_general(flat, weight, (((1,), (1,)), ((), ())), preferred_element...]
    psum x1 -> x0, waiting for transfers between devices: 32.7 us -> none  [on_device(): lax.psum(grad_part.astype(jnp.bfloat16), 'tensor').astype(jnp.float32)]
    all_to_all x1 -> x0, waiting for transfers between devices: 9.44 us -> none  [on_device(): lax.all_to_all(hidden_input, 'tensor', split_axis=1, concat_axis=0, tiled...]
    gather x2 -> x0, local copies, waits for them, and re-layouts: 4.32 us -> none  [the longest x1 2.74 us: on_device(): down_block_list = adapter_down[adapter_index]]
    all_to_all x1 -> x0, starting transfers between devices: 4.24 us -> none  [on_device(): lax.all_to_all(hidden_input, 'tensor', split_axis=1, concat_axis=0, tiled...]
  transfers between devices with their start and end apart: 6 -> 0, of which waited for: 6 -> 0; matrix products, arithmetic and copies ran while one was open for 15% -> 0% of each run, Pallas kernels for 0% -> 0%
where the time goes in v1:
time: 86.4 us; the launch traced here: 86.2 us
  Pallas kernels  80.5 us (93%)
  local copies, waits for them, and re-layouts  4.96 us (6%)
    pallas_call x1, Pallas kernels, fused(): pl.pallas_call(kernel, out_shape=(jax.ShapeDtypeStruct((rows, model), BF1...  80.5 us
    unnamed x7, local copies, waits for them, and re-layouts  4.96 us

profile of v1, /device:TPU:0, one launch (start us, length us, event | category | flops | bytes accessed | tf_op | source)
XLA Modules:
  0.0 86.2 jit_solution(6216484369518135967)
XLA Ops:
  0.6 80.5 %shard_map.94 = (bf16[128,5120]{1,0:T(8,128)(2,1)}, f32[128,1280]{1,0:T(8,128)}, f32[128,2048]{1,0:T(8,128)}) custom-call(s32[4]{0:T(128)} %live_ref.1, s32[4]{0:T(128)} %bitcast.9, bf16[128,5120]{1,0:T(8,128)(2,1)} %hid_ref.1, bf16[512,2048]{1,0:T(8,128)(2,1)} %g_ref.1, bf16[5120,2048]{1,0:T(8,128)(2,1)} %w_ref.1, bf16[8,64,1280]{2,1,0:T(8,128)(2,1)} %bitcast.8, ...), custom_call_target="tpu_custom_call" | custom-call | flops 10737418240 | bytes 20971520 | tf_op jit(solution)/shard_map/pallas_call | solution.py:363
  81.2 0.0 copy-start.1
  81.2 2.5 %copy.13 = bf16[128,5120]{1,0:T(8,128)(2,1)} copy(bf16[128,5120]{1,0:T(8,128)(2,1)} %get-tuple-element.12) | data formatting | bytes 2621440
  83.7 0.0 copy-done.1
  83.7 0.0 copy-start
  83.7 0.8 copy.14
  84.6 0.6 copy-done
  85.2 1.0 %copy.15 = f32[2,64,2048]{2,1,0:T(8,128)} copy(f32[2,64,2048]{2,1,0:T(8,128)S(1)} %bitcast.6) | data formatting | bytes 2097152
Async XLA Ops:
  81.2 2.5 %copy-start.1 = (f32[128,1280]{1,0:T(8,128)S(1)}, f32[128,1280]{1,0:T(8,128)}, u32[]{:S(2)}) copy-start(f32[128,1280]{1,0:T(8,128)} %get-tuple-element.7) | copy-start | bytes 1966084
  83.7 1.5 %copy-start = (f32[128,2048]{1,0:T(8,128)S(1)}, f32[128,2048]{1,0:T(8,128)}, u32[]{:S(2)}) copy-start(f32[128,2048]{1,0:T(8,128)} %get-tuple-element.8) | copy-start | bytes 3145732

commit v2 on v1

--- a/solution.py
+++ b/solution.py
@@ -11,7 +11,7 @@
 
 
 adapter_scale = 2.0
-UP_CHUNKS, DOWN_CHUNKS, STEP, WBUFS = 4, 2, 256, 3
+UP_CHUNKS, DOWN_CHUNKS, STEP, WBUFS = 8, 5, 256, 3
 
 
 def dot_nt(a, b):
@@ -29,10 +29,10 @@
 def kernel(
     live_ref, idx_ref, hid_ref, g_ref, w_ref, down_ref, up_ref,
     hg_ref, gd_ref, gu_ref,
-    m_g, w_buf, up_v, down_v, cols, pf, acc, core_s, core_r, y_s, y_r, lora,
-    lg_s, lg_r, la_s, la_r, low_g, low_a, lhs, slots_d, slots_u,
+    m_g, w_buf, up_v, down_v, hid_v, d_s, d_r, term_s, term_r, pf, acc, core_s, core_r, y_s, y_r, lora,
+    lg_s, lg_r, la_r, low_g, low_a, lhs, lhs_d, slots_d, slots_u,
     s1d, s1u, td, tu, xd, xu, s2d, s2u, fd, fu, ids_s, ids_r, sel,
-    loc_sem, w_sem, hs_sem, hr_sem, lgs_sem, lgr_sem, las_sem, lar_sem,
+    loc_sem, w_sem, hs_sem, hr_sem, ts_sem, tr_sem, lgs_sem, lgr_sem, las_sem, lar_sem,
     cs_sem, cr_sem, ys_sem, yr_sem,
     s1_sem, t_sem, x_sem, s2_sem, f_sem, id_sem,
 ):
@@ -57,11 +57,10 @@
     loads = [
         pltpu.make_async_copy(g_ref, m_g, loc_sem.at[0]),
         pltpu.make_async_copy(up_ref, up_v, loc_sem.at[1]),
-        pltpu.make_async_copy(hid_ref.at[:, pl.ds(pl.multiple_of(t * width, 128), width)],
-                              cols.at[pl.ds(pl.multiple_of(t * BLOCK, BLOCK), BLOCK), :], loc_sem.at[2]),
+        pltpu.make_async_copy(hid_ref, hid_v, loc_sem.at[2]),
         pltpu.make_async_copy(down_ref, down_v, loc_sem.at[3]),
     ]
-    for x in loads[:2]:
+    for x in (loads[3], loads[0], loads[1], loads[2]):
         x.start()
 
     def w_load(j):
@@ -70,8 +69,6 @@
         )
 
     w_load(0).start()
-    loads[2].start()
-    loads[3].start()
     for j in range(1, WBUFS):
         w_load(j).start()
 
@@ -98,15 +95,18 @@
     def rows_of(b):
         return pl.ds(pl.multiple_of(b * BLOCK, BLOCK), BLOCK)
 
-    def hid_copy(r, sender):
-        p = lax.rem(t + r, 4)
+    def down_copy(r):
+        return remote(d_s.at[r - 1], d_r.at[r - 1], hs_sem.at[r], hr_sem.at[r], {"tensor": lax.rem(t + r, 4)})
+
+    def term_copy(r, sender):
         return remote(
-            hid_ref.at[:, pl.ds(pl.multiple_of(p * width, 128), width)],
-            cols.at[rows_of(sender), :], hs_sem.at[r], hr_sem.at[r], {"tensor": p},
+            term_s.at[r - 1], term_r.at[sender], ts_sem.at[r], tr_sem.at[r], {"tensor": lax.rem(t + r, 4)}
         )
 
-    for r in range(1, 4):
-        hid_copy(r, t).start()
+    loads[3].wait()
+    for r in (2, 3, 1):
+        d_s[r - 1] = down_v[idx_ref[lax.rem(t + r, 4)]]
+        down_copy(r).start()
 
     lane = lax.broadcasted_iota(jnp.int32, ids_s.shape, 1) // rank
     ids = jnp.zeros(ids_s.shape, F32)
@@ -132,16 +132,19 @@
     for r in range(1, 4):
         low_copy(lg_s, lg_r, lgs_sem, lgr_sem, r).start()
 
-    def partial(j):
-        w_load(j).wait()
+    def partial(j, begin=0, end=None):
+        last = width // STEP
+        end = last if end is None else end
+        if begin == 0:
+            w_load(j).wait()
 
         def body(n, carry):
             at = pl.ds(pl.multiple_of(n * STEP, STEP), STEP)
             pf[j % 2, :, at] = dot_nt(m_g[...], w_buf[j % WBUFS, at, :])
             return carry
 
-        lax.fori_loop(0, width // STEP, body, 0)
-        if j + WBUFS < 4:
+        lax.fori_loop(begin, end, body, 0)
+        if end == last and j + WBUFS < 4:
             w_load(j + WBUFS).start()
 
     def core_copy(j):
@@ -168,28 +171,35 @@
         acc[:, pl.ds(j * width, width)] = pf[j % 2, rows_of(y * 2 + c), :] + core_r[j, y].astype(F32)
 
     partial(0)
-    partial(1)
+
+    def hid_cols(p):
+        return hid_v[:, pl.ds(pl.multiple_of(p * width, 128), width)]
+
+    loads[2].wait()
+    mine = dot_nt(down_v[idx_ref[t]], hid_cols(t))
+    for r in range(1, 4):
+        down_copy(r).wait_recv()
+        mine = mine + dot_nt(d_r[r - 1], hid_cols(lax.rem(t + 4 - r, 4)))
+    low_a[:, rows_of(t)] = mine.astype(BF16)
+
+    def act_copy(r):
+        return remote(
+            low_a.at[:, rows_of(t)], la_r.at[r - 1], las_sem.at[r], lar_sem.at[r], {"tensor": lax.rem(t + r, 4)}
+        )
+
+    for r in range(1, 4):
+        act_copy(r).start()
 
     for r in range(1, 4):
         low_copy(lg_s, lg_r, lgs_sem, lgr_sem, r).wait_recv()
     low_g[...] = (
         lg_s[...].astype(F32) + lg_r[0].astype(F32) + lg_r[1].astype(F32) + lg_r[2].astype(F32)
     ).astype(BF16)
-    loads[3].wait()
-    for b in range(nb):
-        at = pl.ds(b * BLOCK, BLOCK)
-        lora[at, :] = (adapter_scale * dot_tn(low_g[:, at], down_v[idx_ref[b]])).astype(BF16)
-    send_core(0)
-    send_core(1)
-
-    loads[2].wait()
-    for r in range(1, 4):
-        hid_copy(r, lax.rem(t + 4 - r, 4)).wait_recv()
-    for b in range(nb):
-        at = pl.ds(b * BLOCK, BLOCK)
-        la_s[:, at] = dot_nt(down_v[idx_ref[b]], cols[at, :]).astype(BF16)
-    for r in range(1, 4):
-        low_copy(la_s, la_r, las_sem, lar_sem, r).start()
+    own_low = (adapter_scale * low_g[:, rows_of(t)].astype(F32)).astype(BF16)
+    for r in (2, 3, 1):
+        term_s[r - 1] = dot_nn(own_low, hid_cols(lax.rem(t + r, 4))).astype(BF16)
+        term_copy(r, t).start()
+    term_r[t] = dot_nn(own_low, hid_cols(t)).astype(BF16)
 
     end_f = is_end.astype(F32)
 
@@ -202,24 +212,42 @@
             return d * own + (s - 2 * own)
         return outer * own + (s - 3 * own)
 
-    def fill(low):
+    def share(s, b):
+        same = (idx_ref[b] == adapter_of(s)).astype(F32)
+        if s < 2 * own:
+            same = end_f * (1.0 if s == b else 0.0) + (1.0 - end_f) * same
+        return same
+
+    eye = (
+        lax.broadcasted_iota(jnp.int32, (rank, nb * rank), 0)
+        == lax.broadcasted_iota(jnp.int32, (rank, nb * rank), 1) % rank
+    ).astype(F32)
+    owner = lax.broadcasted_iota(jnp.int32, (1, nb * rank), 1) // rank
+
+    def fill_up():
         for s in range(4 * own):
             for b in range(nb):
-                same = (idx_ref[b] == adapter_of(s)).astype(F32)
-                if s < 2 * own:
-                    same = end_f * (1.0 if s == b else 0.0) + (1.0 - end_f) * same
                 at = pl.ds(b * BLOCK, BLOCK)
-                lhs[pl.ds(s * rank, rank), at] = (low[:, at].astype(F32) * (adapter_scale * same)).astype(BF16)
+                lhs[pl.ds(s * rank, rank), at] = (
+                    low_a[:, at].astype(F32) * (adapter_scale * share(s, b))
+                ).astype(BF16)
+
+    def fill_down():
+        for s in range(4 * own):
+            row = jnp.zeros((1, nb * rank), F32)
+            for b in range(nb):
+                row = row + (owner == b).astype(F32) * share(s, b)
+            lhs_d[pl.ds(s * rank, rank), :] = (eye * row).astype(BF16)
 
     NC = DOWN_CHUNKS + UP_CHUNKS
 
     def pick(k, down, up):
-        return down.at[k] if k < DOWN_CHUNKS else up.at[k - DOWN_CHUNKS]
+        return down.at[k - UP_CHUNKS] if k >= UP_CHUNKS else up.at[k]
 
     def slot_at(k):
-        if k < DOWN_CHUNKS:
-            return slots_d, pl.ds(k * dw, dw)
-        return slots_u, pl.ds((k - DOWN_CHUNKS) * uw, uw)
+        if k >= UP_CHUNKS:
+            return slots_d, pl.ds((k - UP_CHUNKS) * dw, dw)
+        return slots_u, pl.ds(k * uw, uw)
 
     def end_copy(k):
         return remote(pick(k, s1d, s1u), pick(k, td, tu), s1_sem.at[k], t_sem.at[k], {"dp": inner})
@@ -234,8 +262,11 @@
 
     def local_terms(k):
         slots, at = slot_at(k)
-        right = cols if k < DOWN_CHUNKS else m_g
-        slots[:, at] = dot_nn(lhs[...], right[:, at])
+        if k >= UP_CHUNKS:
+            right = jnp.concatenate([term_r[b, :, at] for b in range(nb)], axis=0)
+            slots[:, at] = dot_nn(lhs_d[...], right)
+        else:
+            slots[:, at] = dot_nn(lhs[...], m_g[:, at])
 
         @pl.when(is_end)
         def _():
@@ -255,7 +286,7 @@
 
     def middle_out(k):
         slots, at = slot_at(k)
-        out = gd_ref if k < DOWN_CHUNKS else gu_ref
+        out = gd_ref if k >= UP_CHUNKS else gu_ref
 
         @pl.when(is_mid)
         def _():
@@ -267,54 +298,67 @@
 
     def end_out(k):
         slots, at = slot_at(k)
-        out = gd_ref if k < DOWN_CHUNKS else gu_ref
+        out = gd_ref if k >= UP_CHUNKS else gu_ref
 
         @pl.when(is_end)
         def _():
             outer_copy(k).wait_recv()
             out[:, at] = slots[half:out_rows, at] + pick(k, fd, fu)[...].astype(F32)
 
-    fill(low_g)
-    for k in range(DOWN_CHUNKS):
-        local_terms(k)
-    combine(0)
-    combine(1)
-    partial(2)
-    send_core(2)
-
-    for r in range(1, 4):
-        low_copy(la_s, la_r, las_sem, lar_sem, r).wait_recv()
-    low_a[...] = (
-        la_s[...].astype(F32) + la_r[0].astype(F32) + la_r[1].astype(F32) + la_r[2].astype(F32)
-    ).astype(BF16)
-    fill(low_a)
-    for k in range(DOWN_CHUNKS, NC):
+    for r in range(1, 4):
+        act_copy(r).wait_recv()
+        low_a[:, rows_of(lax.rem(t + 4 - r, 4))] = la_r[r - 1]
+    fill_up()
+    for k in range(UP_CHUNKS):
         local_terms(k)
 
     @pl.when(is_mid)
     def _():
         remote(ids_s, ids_r, id_sem.at[0], id_sem.at[1], {"dp": cross}).wait_recv()
-        eye = lax.broadcasted_iota(jnp.int32, (rank, nb * rank), 0) == (
-            lax.broadcasted_iota(jnp.int32, (rank, nb * rank), 1) % rank
-        )
-        eye = eye.astype(F32)
         for s in range(3 * own):
             same = (ids_r[0:1, :] == adapter_of(s).astype(F32)).astype(F32)
             sel[pl.ds(s * rank, rank), :] = (eye * same).astype(BF16)
 
-    for k in range(DOWN_CHUNKS):
+    for b in range(nb):
+        at = pl.ds(b * BLOCK, BLOCK)
+        lora[at, :] = (adapter_scale * dot_tn(low_g[:, at], down_v[idx_ref[b]])).astype(BF16)
+    send_core(0)
+    middle_sums(0)
+    partial(1, 0, 3)
+    middle_sums(1)
+    partial(1, 3)
+    send_core(1)
+    combine(0)
+    middle_sums(2)
+    fill_down()
+    for r in range(1, 4):
+        term_copy(r, lax.rem(t + 4 - r, 4)).wait_recv()
+    for k in range(UP_CHUNKS, NC):
+        local_terms(k)
+    middle_sums(3)
+    middle_out(0)
+    partial(2, 0, 3)
+    middle_sums(4)
+    middle_out(1)
+    combine(1)
+    partial(2, 3)
+    send_core(2)
+    middle_sums(5)
+    middle_out(2)
+    partial(3, 0, 3)
+    middle_sums(6)
+    middle_out(3)
+    combine(2)
+    partial(3, 3)
+    send_core(3)
+    middle_sums(7)
+    middle_out(4)
+    combine(3)
+    for k in range(UP_CHUNKS, NC):
         middle_sums(k)
-    combine(2)
-    partial(3)
-    send_core(3)
-    middle_sums(DOWN_CHUNKS)
-    combine(3)
-    for k in range(DOWN_CHUNKS):
+        middle_out(k - 3)
+    for k in range(NC - 3, NC):
         middle_out(k)
-    for k in range(DOWN_CHUNKS + 1, NC):
-        middle_sums(k)
-        middle_out(k - 1)
-    middle_out(NC - 1)
     for j in range(4):
         at = pl.ds(j * width, width)
         y_copy(j).wait_recv()
@@ -323,9 +367,10 @@
         end_out(k)
 
     for r in range(1, 4):
-        hid_copy(r, t).wait_send()
+        down_copy(r).wait_send()
+        term_copy(r, t).wait_send()
         low_copy(lg_s, lg_r, lgs_sem, lgr_sem, r).wait_send()
-        low_copy(la_s, la_r, las_sem, lar_sem, r).wait_send()
+        act_copy(r).wait_send()
     for j in range(4):
         core_copy(j).wait_send()
         y_copy(j).wait_send()
@@ -374,7 +419,11 @@
             V((WBUFS, width, q), BF16),
             V((na, rank, q), BF16),
             V((na, rank, width), BF16),
-            V((group, width), BF16),
+            V((rows, model), BF16),
+            V((3, rank, width), BF16),
+            V((3, rank, width), BF16),
+            V((3, rank, width), BF16),
+            V((nt, rank, width), BF16),
             V((2, group, width), F32),
             V((rows, model), F32),
             V((nt, 2, rows, width), BF16),
@@ -384,17 +433,17 @@
             V((group, width), BF16),
             V((rank, group), BF16),
             V((3, rank, group), BF16),
-            V((rank, group), BF16),
-            V((3, rank, group), BF16),
+            V((3, rank, rows), BF16),
             V((rank, group), BF16),
             V((rank, group), BF16),
             V((na * rank, group), BF16),
+            V((na * rank, nt * rank), BF16),
             V((na * rank, width), F32),
             V((na * rank, q), F32),
         ]
         + pair(half) + pair(half) + pair(half) + pair(mine) + pair(mine)
         + [V((8, nt * rank), F32), V((8, nt * rank), F32), V((3 * mine, nt * rank), BF16)]
-        + [S((n,)) for n in (4, 4, 4, 4, 4, 4, 4, 4, 4, 4, 4, 4, nc, nc, nc, nc, nc, 2)],
+        + [S((n,)) for n in (4, 4, 4, 4, 4, 4, 4, 4, 4, 4, 4, 4, 4, 4, nc, nc, nc, nc, nc, 2)],
         compiler_params=pltpu.CompilerParams(
             collective_id=0, has_side_effects=True, vmem_limit_bytes=62 * 1024 * 1024
         ),

time: 86.4 us -> 73.2 us (0.85)
  Pallas kernels: 80.5 us -> 67.4 us
    pallas_call x1, Pallas kernels: 80.5 us -> 67.4 us  [fused(): pl.pallas_call(kernel, out_shape=(jax.ShapeDtypeStruct((rows, model), BF1...]
where the time goes in v2:
time: 73.2 us; the launch traced here: 73 us
  Pallas kernels  67.4 us (92%)
  local copies, waits for them, and re-layouts  4.96 us (7%)
    pallas_call x1, Pallas kernels, fused(): pl.pallas_call(kernel, out_shape=(jax.ShapeDtypeStruct((rows, model), BF1...  67.4 us
    unnamed x7, local copies, waits for them, and re-layouts  4.96 us

profile of v2, /device:TPU:0, one launch (start us, length us, event | category | flops | bytes accessed | tf_op | source)
XLA Modules:
  0.0 73.0 jit_solution(11642871286028662507)
XLA Ops:
  0.6 67.4 %shard_map.94 = (bf16[128,5120]{1,0:T(8,128)(2,1)}, f32[128,1280]{1,0:T(8,128)}, f32[128,2048]{1,0:T(8,128)}) custom-call(s32[4]{0:T(128)} %live_ref.1, s32[4]{0:T(128)} %bitcast.9, bf16[128,5120]{1,0:T(8,128)(2,1)} %hid_ref.1, bf16[512,2048]{1,0:T(8,128)(2,1)} %g_ref.1, bf16[5120,2048]{1,0:T(8,128)(2,1)} %w_ref.1, bf16[8,64,1280]{2,1,0:T(8,128)(2,1)} %bitcast.8, ...), custom_call_target="tpu_custom_call" | custom-call | flops 10737418240 | bytes 20971520 | tf_op jit(solution)/shard_map/pallas_call | solution.py:408
  68.0 0.0 copy-start.1
  68.0 2.5 %copy.13 = bf16[128,5120]{1,0:T(8,128)(2,1)} copy(bf16[128,5120]{1,0:T(8,128)(2,1)} %get-tuple-element.12) | data formatting | bytes 2621440
  70.6 0.0 copy-done.1
  70.6 0.0 copy-start
  70.6 0.8 %copy.14 = f32[2,1280,64]{1,2,0:T(8,128)} copy(f32[2,1280,64]{1,2,0:T(8,128)S(1)} %bitcast.7) | data formatting | bytes 1310720
  71.4 0.6 copy-done
  72.0 1.0 %copy.15 = f32[2,64,2048]{2,1,0:T(8,128)} copy(f32[2,64,2048]{2,1,0:T(8,128)S(1)} %bitcast.6) | data formatting | bytes 2097152
Async XLA Ops:
  68.0 2.5 %copy-start.1 = (f32[128,1280]{1,0:T(8,128)S(1)}, f32[128,1280]{1,0:T(8,128)}, u32[]{:S(2)}) copy-start(f32[128,1280]{1,0:T(8,128)} %get-tuple-element.7) | copy-start | bytes 1966084
  70.6 1.5 %copy-start = (f32[128,2048]{1,0:T(8,128)S(1)}, f32[128,2048]{1,0:T(8,128)}, u32[]{:S(2)}) copy-start(f32[128,2048]{1,0:T(8,128)} %get-tuple-element.8) | copy-start | bytes 3145732
